TPU v7x, 128 devices: a whole 4x4x4 slice. The times are simulated.
128 devices in a mesh: dp: 4 (over z_lo, core), ctx: 32 (over y, x, z_hi).
Axes of the slice: x: 4, y: 4, z: 4 (z_hi: 2, z_lo: 2; z = z_hi * 2 + z_lo), core: 2. Of those that a mesh axis runs over, the one named last changes fastest.
Arguments:
- tokens_in: bfloat16 [4, 4096, 1536], P('dp', 'ctx'), may hold values from -6 to 6
- qkv_weight: bfloat16 [2048, 1536], P(('dp', 'ctx')), may hold values from -0.21875 to 0.21875
- qkv_bias: bfloat16 [2048], P(('dp', 'ctx')), may hold values from -3 to 3
- out_weight: bfloat16 [1536, 1536], P(('dp', 'ctx')), may hold values from -0.625 to 0.625
- norm_gains: bfloat16 [2, 1536], P(None, ('dp', 'ctx')), may hold values from 0.099609375 to 1.8984375
- gate_weight: bfloat16 [8960, 1536], P(('dp', 'ctx')), may hold values from -0.15625 to 0.15625
- up_weight: bfloat16 [8960, 1536], P(('dp', 'ctx')), may hold values from -0.15625 to 0.15625
- down_weight: bfloat16 [8960, 1536], P(('dp', 'ctx')), may hold values from -0.125 to 0.125
- doc_ids: int32 [4, 4096], P('dp'), may hold values from 0 to 2, as said below
- cotangent: bfloat16 [4, 4096, 1536], P('dp', 'ctx'), may hold values from -6 to 6
Outputs:
- layer_out: bfloat16 [4, 4096, 1536], P('dp', 'ctx')
- input_grad: float32 [4, 4096, 1536], P('dp', 'ctx')
- qkv_weight_grad: float32 [2048, 1536], P(('dp', 'ctx'))
- qkv_bias_grad: float32 [2048], P(('dp', 'ctx'))
- out_weight_grad: float32 [1536, 1536], P(('dp', 'ctx'))
- norm_gains_grad: float32 [2, 1536], P(None, ('dp', 'ctx'))
- gate_weight_grad: float32 [8960, 1536], P(('dp', 'ctx'))
- up_weight_grad: float32 [8960, 1536], P(('dp', 'ctx'))
- down_weight_grad: float32 [8960, 1536], P(('dp', 'ctx'))
Inputs may be any that keep to these rules, and one draw needn't show every extreme that they name: `doc_ids`: in every sequence the ids never fall and take exactly the values 0, 1, 2; document 1 begins within the first half of 128 tokens and ends within the last half of 128 tokens; documents 0 and 2 are not empty.
All inputs are finite; a program needn't handle non-finite values.
Results may differ from a plain program's by a relative error of at most 0.033.
Values may be sent and summed in bfloat16 or wider, within the bound.
A program may use at most 512 MiB of HBM per device.

v0:
```python
import math

import jax
import jax.numpy as jnp
from jax import lax
from jax.experimental import pallas as pl
from jax.experimental.pallas import tpu as pltpu
from jax.sharding import Mesh
from jax.sharding import PartitionSpec as P

H = 12
KVH = 2
HD = 128
HQ = 1536
D = 1536
TOK = 128
ROWS = 80

norm_eps = 1e-06
rope_base = 1000000.0

AXES = ("zl", "c", "y", "x", "zh")
SIZE = {"zl": 2, "c": 2, "y": 4, "x": 4, "zh": 2}
PARTS_OF = {"z": ("zl", "zh"), "x": ("x",), "y": ("y",), "c": ("c",), "zh": ("zh",)}
REACH = {"z": (1, 2, 3), "x": (1, 2, 3), "y": (1, 2, 3), "c": (1,), "zh": (1,)}
BF = jnp.bfloat16
F32 = jnp.float32
ANY = pl.BlockSpec(memory_space=pl.ANY)
VMEM = pl.BlockSpec(memory_space=pltpu.VMEM)


def here():
    return {a: lax.axis_index(a) for a in AXES}


def peer(me, axis, k):
    to = dict(me)
    if axis == "z":
        z = lax.rem(me["zh"] * 2 + me["zl"] + k, 4)
        to["zl"], to["zh"] = lax.rem(z, 2), lax.div(z, 2)
    else:
        to[axis] = lax.rem(me[axis] + k, SIZE[axis])
    return to


def device_id(at):
    return tuple(at[a] for a in AXES)


def place(dims, at, whole, tail=()):
    return tuple(slice(None) if d in whole else at[d] for d in dims) + tuple(tail)


class Links:
    def __init__(self, me, send, recv):
        self.me, self.send, self.recv, self.used = me, send, recv, 0

    def copy(self, src, dst, axis, k):
        i = self.used
        self.used += 1
        c = pltpu.make_async_remote_copy(
            src_ref=src,
            dst_ref=dst,
            send_sem=self.send.at[i],
            recv_sem=self.recv.at[i],
            device_id=device_id(peer(self.me, axis, k)),
            device_id_type=pl.DeviceIdType.MESH,
        )
        c.start()
        return c


def greet(me, axes):
    barrier = pltpu.get_barrier_semaphore()
    count = 0
    for axis in axes:
        for k in REACH[axis]:
            pl.semaphore_signal(
                barrier,
                inc=1,
                device_id=device_id(peer(me, axis, k)),
                device_id_type=pl.DeviceIdType.MESH,
            )
            count += 1
    pl.semaphore_wait(barrier, count)


def halves_of(tail, cols):
    rows = tail[:-1] if tail else (slice(None),)
    start = tail[-1].start if tail else 0
    cut = cols // 2
    return tuple(rows + (slice(start + cut * i, start + cut * (i + 1)),) for i in range(2))


def gather_stream(links, block, buf, dims, tail, order):
    me = links.me
    whole = ()
    cols = block.shape[-1]
    for n, axis in enumerate(order):
        direct = axis.endswith("!")
        axis = axis.rstrip("!")
        mine = place(dims, me, whole, tail)
        src = block if n == 0 else buf.at[mine]
        ring = len(REACH[axis]) == 3 and not direct
        near = (1, 3) if ring else REACH[axis]
        copies = [links.copy(src, buf.at[mine], axis, k) for k in near]
        yield
        for c in copies:
            c.wait()
        if ring:
            copies = []
            for k, half in zip(near, halves_of(tail, cols), strict=True):
                theirs = buf.at[place(dims, peer(me, axis, 4 - k), whole, half)]
                copies.append(links.copy(theirs, theirs, axis, k))
            yield
            for c in copies:
                c.wait()
        whole = whole + PARTS_OF[axis]


def run_streams(streams):
    live = list(streams)
    while live:
        live = [s for s in live if next(s, live) is not live]


def step(streams):
    for s in streams:
        next(s, None)


def count_gather(orders):
    return sum({"c": 1, "zh": 1}.get(a, 3 if "!" in a else 4) for order in orders for a in order)


def count_scatter(orders):
    return sum(4 if "~" in a else len(REACH[a]) for order in orders for a in order)


THIRDS = tuple((slice(None), slice(512 * i, 512 * (i + 1))) for i in range(3))
ORDERS = (("x", "y", "z"), ("y", "z", "x"), ("z", "x", "y"))


def cut_at(column):
    return ((slice(None), slice(0, column)), (slice(None), slice(column, D)))


HALVES = cut_at(768)
GATHER_CUTS = (1024, 768, 1024)
THIRD_ORDERS = (("y", "z"), ("z", "y"), ("z", "y"))
FFN_ORDERS = (("y", "z"), ("z", "y"))
FFN_DIMS = ("zl", "y", "zh")
ROW_DIMS = ("x", "c")
KV_DIMS = ("y", "x", "zh")


def lead_of(dims):
    return tuple(SIZE[d] for d in dims)


def rest_of(dims, axis):
    return tuple(d for d in dims if d not in PARTS_OF[axis])


def scatter_scratch(dims, order, rows, cols):
    shapes = []
    for axis in order:
        ring = axis.endswith("~")
        axis = axis.rstrip("~")
        dims = rest_of(dims, axis)
        block = lead_of(dims) + (rows, cols)
        shapes.append(pltpu.VMEM((2 if ring else len(REACH[axis]),) + block, BF))
        shapes.append(pltpu.VMEM(block, BF))
        if ring:
            shapes.append(pltpu.VMEM((2,) + lead_of(dims) + (rows, cols // 2), BF))
            shapes.append(pltpu.VMEM((2,) + block, BF))
    return shapes


def block_index(i, lead, rows, step):
    per = rows // step
    block, row = lax.div(i, per), lax.rem(i, per)
    fine = lead[-1:] == (2,)
    index = []
    for n in reversed(lead[:-1] if fine else lead):
        index.append(lax.rem(block, n))
        block = lax.div(block, n)
    at = tuple(reversed(index)) + ((slice(None),) if fine else ())
    return at + (pl.ds(pl.multiple_of(row * step, step), step),)


def step_count(lead, rows, step):
    count = rows // step
    for n in lead[:-1] if lead[-1:] == (2,) else lead:
        count *= n
    return count


def sum_blocks(own, arrived, out, lead, rows, step):
    parts = arrived.shape[0]

    def body(i, carry):
        at = block_index(i, lead, rows, step)
        total = own[at].astype(F32)
        for p in range(parts):
            total = total + arrived[(p,) + at].astype(F32)
        out[at] = total.astype(out.dtype)
        return carry

    lax.fori_loop(0, step_count(lead, rows, step), body, 0)


def add_blocks(total, part, lead, rows, step, cols):
    def body(i, carry):
        at = block_index(i, lead, rows, step)
        whole = total[at + (cols,)].astype(F32) + part[at + (slice(None),)].astype(F32)
        total[at + (cols,)] = whole.astype(BF)
        return carry

    lax.fori_loop(0, step_count(lead, rows, step), body, 0)


def scatter_stream(links, local, source, dims, tail, order, scratch, out, rows, step):
    me = links.me
    now = None
    scratch = list(scratch)
    for n, axis in enumerate(order):
        ring = axis.endswith("~")
        axis = axis.rstrip("~")
        arrived, own = scratch.pop(0), scratch.pop(0)
        gone = PARTS_OF[axis]
        keep = tuple(d for d in dims if d not in gone)
        lead = lead_of(keep)
        end = tail if n == 0 else ()
        base = source if n == 0 else now
        staged = n == 0 and local is not None
        held = base.at[place(dims, me, keep, end)]
        fetched = []

        def stage(src, dst, sem):
            fetched.append(pltpu.make_async_copy(src, dst, sem))
            fetched[-1].start()

        if ring:
            passed, onward = scratch.pop(0), scratch.pop(0)
            cut = passed.shape[-1]
            copies = []
            for i, k in enumerate((1, 3)):
                half = halves_of(end, 2 * cut)[i]
                src = base.at[place(dims, peer(me, axis, 2), keep, half)]
                copies.append(links.copy(src, passed.at[i], axis, k))
                src = base.at[place(dims, peer(me, axis, k), keep, end)]
                if staged:
                    stage(src, onward.at[i], local.at[i])
            if staged:
                stage(held, own, local.at[2])
                held = own
            yield
            for c in fetched + copies:
                c.wait()
            copies = []
            for i, k in enumerate((1, 3)):
                cols = pl.ds(cut * i, cut)
                to = onward.at[i]
                add_blocks(to, passed.at[i], lead, rows, step, cols)
                copies.append(links.copy(to, arrived.at[i], axis, k))
        else:
            copies = []
            for k in REACH[axis]:
                src = base.at[place(dims, peer(me, axis, k), keep, end)]
                copies.append(links.copy(src, arrived.at[k - 1], axis, k))
            if staged:
                stage(held, own, local)
                held = own
        yield
        for c in ([] if ring else fetched) + copies:
            c.wait()
        target = out if n == len(order) - 1 else own
        sum_blocks(held, arrived, target, lead, rows, step)
        now, dims = own, keep


FIRST_STAGE = (("y~",), ("z~",))
LAST_STAGE = (("z",), ("y",))
KV_ORDERS = (("y", "x", "zh"), ("x", "y", "zh"))
ALL_ORDERS = tuple(("c",) + o for o in ORDERS)


def rows_scatter_kernel(*refs):
    middle, cot, gains, slots = refs[:4]
    rows, tokens, cots, hidden, gate, up, w_out = refs[4:11]
    middle_grad, gain_two_grad, grad_slots, sum_a, sum_b = refs[11:16]
    gate_part, up_part, out_part = refs[16:19]
    out, weight, tokens_v, cots_v, lhs, part, down, out_v, send, recv, local = refs[19:30]
    scratch = refs[30:]
    me = here()
    links = Links(me, send, recv)
    used = [0]

    def move(src, dst):
        used[0] += 1
        c = pltpu.make_async_copy(src, dst, local.at[used[0] - 1])
        c.start()
        return c

    first = [move(hidden, lhs.at[0]), move(cots, cots_v)]
    second = [move(gate, lhs.at[1]), move(tokens, tokens_v)]
    fetched = move(w_out, weight)
    greet(me, ("x", "y", "z", "c"))
    streams = [
        scatter_stream(links, local.at[20], rows, ROW_DIMS, (), ("c", "x"), scratch[8:], out, TOK, 16)
    ]
    step(streams)

    def product(left, right, result):
        def body(i, carry):
            at = pl.ds(pl.multiple_of(i * 4 * ROWS, 4 * ROWS), 4 * ROWS)
            for j in range(3):
                cols = slice(512 * j, 512 * (j + 1))
                block = mm(left[at], right[:, cols], (1, 0)).astype(BF)
                result[lax.div(i, 2), pl.ds(lax.rem(i, 2) * 2, 2), :, :, cols] = block.reshape(
                    2, 2, ROWS, 512
                )
            return carry

        lax.fori_loop(0, 4, body, 0)

    for c in first:
        c.wait()
    product(lhs.at[0], cots_v, down)
    step(streams)
    weights = [
        scatter_stream(
            links,
            local.at[pl.ds(21 + 3 * i, 3)],
            down,
            FFN_DIMS,
            HALVES[i],
            FIRST_STAGE[i],
            scratch[4 * i : 4 * i + 4],
            (sum_a, sum_b)[i],
            ROWS,
            16,
        )
        for i in range(2)
    ]
    step(weights)
    third = move(up, lhs.at[0])
    for c in second:
        c.wait()
    product(lhs.at[1], tokens_v, part.at[0])
    stored = [move(part.at[0], gate_part)]
    step(weights)
    third.wait()
    product(lhs.at[0], tokens_v, part.at[1])
    stored.append(move(part.at[1], up_part))
    turned_slots = jnp.concatenate(
        [slots[:, head(i)].astype(F32).T.astype(BF) for i in range(16)], axis=0
    )
    step(streams)
    grad = out[...]
    mid = middle[...]
    factor = lax.rsqrt(jnp.sum(mid * mid, axis=1, keepdims=True) / D + norm_eps)
    gain_two_grad[...] = jnp.sum(grad * mid * factor, axis=0, keepdims=True)
    scaled = grad * gains[8:9]
    mean = jnp.sum(scaled * mid, axis=1, keepdims=True) / D
    total = cot[...].astype(F32) + factor * scaled - mid * (factor * factor * factor * mean)
    middle_grad[...] = total
    branch = total.astype(BF)
    fetched.wait()
    for i in range(4):
        grad_slots[:, 512 * i : 512 * (i + 1)] = mm(
            branch, weight[512 * i : 512 * (i + 1)], (1, 1)
        ).astype(BF)
    for i in range(4):
        for j in range(3):
            cols = slice(512 * j, 512 * (j + 1))
            block = mm(turned_slots[512 * i : 512 * (i + 1)], branch[:, cols], (1, 0))
            out_v[i // 2, i % 2, :, :, :, :, cols] = block.astype(BF).reshape(4, 4, 2, 16, 512)
        stored.append(move(out_v.at[i // 2, i % 2], out_part.at[i // 2, i % 2]))
    step(weights)
    for c in stored:
        c.wait()


def scatter_rows(own, rows, tokens, cots, hidden, gate, up, w_out):
    copies = count_scatter([("c", "x")]) + count_scatter(FIRST_STAGE)
    lead = lead_of(FFN_DIMS) + (ROWS, D)
    every = lead_of(AXES) + (16, D)
    scratch, sums = [], []
    for order in FIRST_STAGE:
        scratch += scatter_scratch(FFN_DIMS, order, ROWS, 768)
        rest = rest_of(FFN_DIMS, order[0].rstrip("~"))
        sums.append(jax.ShapeDtypeStruct(lead_of(rest) + (ROWS, 768), BF))
    part = jax.ShapeDtypeStruct(lead, BF)
    return pl.pallas_call(
        rows_scatter_kernel,
        out_shape=(
            jax.ShapeDtypeStruct((TOK, D), F32),
            jax.ShapeDtypeStruct((1, D), F32),
            jax.ShapeDtypeStruct((TOK, 2048), BF),
            *sums,
            part,
            part,
            jax.ShapeDtypeStruct(every, BF),
        ),
        in_specs=[VMEM] * 4 + [ANY] * 7,
        out_specs=(VMEM,) * 5 + (ANY,) * 3,
        scratch_shapes=[
            pltpu.VMEM((TOK, D), F32),
            pltpu.VMEM((2048, D), BF),
            pltpu.VMEM(tokens.shape, BF),
            pltpu.VMEM(cots.shape, BF),
            pltpu.VMEM((2,) + hidden.shape, BF),
            pltpu.VMEM((2,) + lead, BF),
            pltpu.VMEM(lead, BF),
            pltpu.VMEM(every, BF),
            pltpu.SemaphoreType.DMA((copies,)),
            pltpu.SemaphoreType.DMA((copies,)),
            pltpu.SemaphoreType.DMA((27,)),
        ]
        + scratch
        + scatter_scratch(ROW_DIMS, ("c", "x"), TOK, D),
        compiler_params=pltpu.CompilerParams(
            collective_id=4, has_side_effects=True, vmem_limit_bytes=63 * 2**20
        ),
    )(*own, rows, tokens, cots, hidden, gate, up, w_out)


GROUP = H // KVH
GQ = GROUP * TOK
KEYS = 512
SCALE = HD**-0.5
TO_LOG2 = SCALE * math.log2(math.e)


def head(h):
    return slice(128 * h, 128 * (h + 1))


def turned(v):
    return pltpu.roll(v, 64, 1)


def key_blocks():
    ctx = lax.axis_index("y") * 8 + lax.axis_index("x") * 2 + lax.axis_index("zh")
    return lax.div(ctx, 4) + 1, ctx * TOK


def key_block_of(ref, b, cols):
    return ref[lax.div(b, 2), pl.ds(lax.rem(b, 2) * 2, 2), :, :, cols].reshape(KEYS, HD)


def allowed_keys(b, first, row):
    key = b * KEYS + lax.broadcasted_iota(jnp.int32, (KEYS, GQ), 0)
    query = row + lax.rem(lax.broadcasted_iota(jnp.int32, (1, GQ), 1), TOK)
    return (key <= query) & (key >= first)


def over_key_blocks(blocks, body):
    def at_edge(i, carry):
        body(i * (blocks - 1), True)
        return carry

    def between(b, carry):
        body(b, False)
        return carry

    lax.fori_loop(0, jnp.minimum(blocks, 2), at_edge, 0)
    lax.fori_loop(1, blocks - 1, between, 0)


def mm(a, b, contract):
    return lax.dot_general(
        a, b, ((contract[:1], contract[1:]), ((), ())), preferred_element_type=F32
    )


def attend_all(kv, qs, first, row, blocks, acc, stats):
    acc[...] = jnp.zeros_like(acc)
    stats[:, 0:1] = jnp.full((KVH, 1, GQ), -1e30, F32)
    stats[:, 1:2] = jnp.zeros((KVH, 1, GQ), F32)

    def body(b, edge):
        allowed = allowed_keys(b, first, row) if edge else None
        later = jnp.where(first > b * KEYS, -1e30, 0.0)
        for g in range(KVH):
            keys = key_block_of(kv, b, head(g))
            values = key_block_of(kv, b, head(2 + g))
            raw = mm(keys, qs[g], (1, 1)) * TO_LOG2
            raw = jnp.where(allowed, raw, -1e30) if edge else raw + later
            old = stats[g, 0:1]
            top = jnp.maximum(old, jnp.max(raw, axis=0, keepdims=True))
            probs = jnp.exp2(raw - top)
            shrink = jnp.exp2(old - top)
            stats[g, 0:1] = top
            stats[g, 1:2] = stats[g, 1:2] * shrink + jnp.sum(probs, axis=0, keepdims=True)
            acc[g] = acc[g] * shrink + mm(values.T, probs.astype(BF), (1, 0))

    over_key_blocks(blocks, body)


QKV_ORDERS = (("x!", "y!", "z!", "c"), ("y!", "z!", "x!", "c"), ("z!", "x!", "y!", "c"))
OUT_ORDERS = (("y!", "z!", "x", "c"), ("x!", "y!", "z", "c"))
KEY_ORDERS = (("zh", "x!", "y"), ("zh", "y!", "x"))
ROW_ORDER = ("x", "c")


def spread_row(blocks, offset, width, count):
    f = lax.broadcasted_iota(jnp.int32, (1, count), 1).astype(F32)
    block = jnp.floor((f + 0.5) * (1.0 / width))
    lane = offset + f - block * width
    index = lax.broadcasted_iota(jnp.int32, (128, count), 0).astype(F32)
    pick = (index == lane).astype(BF)
    spread = mm(blocks, pick, (1, 0))
    return jnp.sum(jnp.where(index == block, spread, 0.0), axis=0, keepdims=True)


def slot_matrix(out_rows):
    feature = lax.broadcasted_iota(jnp.int32, (384, 512), 0).astype(F32)
    slot = lax.broadcasted_iota(jnp.int32, (384, 512), 1).astype(F32)
    block = jnp.floor((feature + 0.5) * (1.0 / out_rows))
    return (slot == feature + block * (16 - out_rows)).astype(BF)


def position_tables(inverse, documents, cosine, sine, first_ref):
    _, start = key_blocks()
    ids = documents[...]
    counts = [jnp.sum((ids == k).astype(jnp.int32), axis=1, keepdims=True) for k in range(2)]
    mine = documents[:, pl.ds(pl.multiple_of(start, TOK), TOK)]
    first = jnp.where(mine == 0, 0, jnp.where(mine == 1, counts[0], counts[0] + counts[1]))
    first_ref[...] = first
    lane = lax.broadcasted_iota(jnp.int32, (1, TOK), 1)
    position = (start + lane - first).astype(F32)
    angle = jnp.broadcast_to(position, (TOK, TOK)).T * inverse[...]
    cosine[...] = jnp.cos(angle)
    sine[...] = jnp.where(lane < HD // 2, -jnp.sin(angle), jnp.sin(angle))


def front_kernel(*refs):
    tokens, inverse, documents, small, out_in, gate_in, up_in, down_in, cot = refs[:9]
    qkv_block = refs[9]
    normed_one, gains, queries, attended, slots, lse, middle = refs[10:17]
    cosine, sine, first_ref = refs[17:20]
    kv_hbm, qkv_hbm, out_hbm, gate_all, up_all, down_all, cot_all, rows_all = refs[20:28]
    small_all, w_qkv, w_out, kv, out_block, gate, up, down = refs[28:36]
    qkv, block, qs, acc, stats, normed, send, recv, local = refs[36:]
    me = here()
    links = Links(me, send, recv)
    own = []

    def keep(src, dst):
        own.append(pltpu.make_async_copy(src, dst, local.at[len(own)]))
        own[-1].start()
        return own[-1]

    first_copies = [
        keep(qkv_block, w_qkv.at[place(AXES, me, ())]),
        keep(small, small_all.at[place(AXES, me, ())]),
        keep(cot, cot_all.at[place(ROW_DIMS, me, ())]),
    ]
    out_rows = out_in.shape[0]
    out_block[0:out_rows] = out_in[...]
    out_block[out_rows:16] = jnp.zeros((16 - out_rows, D), BF)
    first_copies.append(keep(out_block, w_out.at[place(AXES, me, ())]))
    units = gate_in.shape[0]
    ffn = ((gate_in, gate, gate_all), (up_in, up, up_all), (down_in, down, down_all))
    for a, b, c in ffn:
        b[0:units] = a[...]
        b[units:ROWS] = jnp.zeros((ROWS - units, D), BF)
        first_copies.append(keep(b, c.at[place(FFN_DIMS, me, ())]))
    greet(me, ("x", "y", "z", "c", "zh"))
    qkvs = [
        gather_stream(links, qkv_block.at[tail], w_qkv, AXES, tail, order)
        for order, tail in zip(QKV_ORDERS, THIRDS, strict=True)
    ]
    qkvs.append(gather_stream(links, small, small_all, AXES, (), QKV_ORDERS[1]))
    outs = [
        gather_stream(links, out_block.at[tail], w_out, AXES, tail, order)
        for order, tail in zip(OUT_ORDERS, HALVES, strict=True)
    ]
    by_y, by_z = (
        [
            gather_stream(links, a.at[cut_at(column)[i]], b, FFN_DIMS, cut_at(column)[i], order)
            for (_, a, b), column in zip(ffn, GATHER_CUTS, strict=True)
        ]
        for i, order in enumerate(FFN_ORDERS)
    )
    cots = [gather_stream(links, cot, cot_all, ROW_DIMS, (), ROW_ORDER)]
    step(qkvs)
    step(outs)
    whole = tokens[...].astype(F32)
    factor = lax.rsqrt(jnp.sum(whole * whole, axis=1, keepdims=True) / D + norm_eps)
    first_copies[0].wait()
    first_copies[1].wait()
    step(qkvs)
    position_tables(inverse, documents, cosine, sine, first_ref)
    for c in first_copies[2:]:
        c.wait()
    step(outs)
    step(qkvs)
    step(by_y)
    step(qkvs)
    step(outs)
    step(qkvs)
    saved = [keep(w_qkv, qkv_hbm)]
    row = lax.broadcasted_iota(jnp.int32, (128, 2048), 0)
    entry = lax.broadcasted_iota(jnp.int32, (128, 2048), 1)
    blocks = mm((entry == row * 16).astype(BF), small_all[...].reshape(2048, 128), (1, 0)).astype(BF)
    bias = spread_row(blocks, 0, 16, 2048)
    gain = spread_row(blocks, 16, 12, D)
    gains[0:8] = jnp.broadcast_to(gain, (8, D))
    gain_two = spread_row(blocks, 28, 12, D)
    gains[8:16] = jnp.broadcast_to(gain_two, (8, D))
    normed_one[...] = (tokens[...].astype(F32) * factor * gain).astype(BF)
    cos, sin = cosine[...], sine[...]

    def project(j):
        part = w_qkv[j // 4, (j // 2) % 2, 2 * (j % 2) : 2 * (j % 2) + 2].reshape(256, D)
        return mm(normed_one[...], part, (1, 1)) + bias[:, 256 * j : 256 * (j + 1)]

    part = project(6)
    for g in range(KVH):
        one = part[:, head(g)]
        block[:, head(g)] = (one * cos + turned(one) * sin).astype(BF)
    block[:, 256:512] = project(7).astype(BF)
    mine = keep(block, kv.at[place(KV_DIMS, me, ())])
    keys = []
    for half, order in enumerate(KEY_ORDERS):
        tail = (slice(None), slice(256 * half, 256 * (half + 1)))
        keys.append(gather_stream(links, block.at[tail], kv, KV_DIMS, tail, order))
    step(keys)
    step(by_y)
    step(outs)
    step(by_z)
    mine.wait()
    for j in range(3):
        qkv[:, 256 * j : 256 * (j + 1)] = project(j)
    step(keys)
    for j in range(3, 6):
        qkv[:, 256 * j : 256 * (j + 1)] = project(j)
    step(by_z)
    step(by_y)
    step(keys)
    step(outs)
    for h in range(H):
        one = qkv[:, head(h)]
        rotated = (one * cos + turned(one) * sin).astype(BF)
        queries[:, head(h)] = rotated
        qs[h // GROUP, (h % GROUP) * TOK : (h % GROUP + 1) * TOK, :] = rotated
    step(keys)
    step(by_z)
    step(cots)
    step(keys)
    saved.append(keep(kv, kv_hbm))
    count, start = key_blocks()
    first = jnp.concatenate([first_ref[...]] * GROUP, axis=1)
    attend_all(kv, qs, first, start, count, acc, stats)
    for g in range(KVH):
        total = stats[g, 1:2]
        lse[g] = jnp.broadcast_to(stats[g, 0:1] + jnp.log2(total), (8, GQ))
        for i in range(GROUP):
            attended[:, head(GROUP * g + i)] = (acc[g, :, head(i)] / total[:, head(i)]).T
    step(cots)
    spread = slot_matrix(out_rows)
    for i in range(4):
        part = attended[:, 384 * i : 384 * (i + 1)].astype(BF)
        slots[:, 512 * i : 512 * (i + 1)] = mm(part, spread, (1, 0)).astype(BF)
    step(outs)
    saved.append(keep(w_out, out_hbm))
    square = jnp.zeros((TOK, 1), F32)
    for i in range(3):
        cols = slice(512 * i, 512 * (i + 1))
        part = w_out[:, :, :, :, :, :, cols].reshape(2048, 512)
        part = tokens[:, cols].astype(F32) + mm(slots[...], part, (1, 0))
        middle[:, cols] = part
        square = square + jnp.sum(part * part, axis=1, keepdims=True)
    factor = lax.rsqrt(square / D + norm_eps)
    normed[...] = (middle[...] * factor * gains[8:9]).astype(BF)
    mine = keep(normed, rows_all.at[place(ROW_DIMS, me, ())])
    rows = [gather_stream(links, normed, rows_all, ROW_DIMS, (), ROW_ORDER)]
    step(rows)
    step(by_y)
    step(by_z)
    step(cots)
    mine.wait()
    step(rows)
    step(rows)
    step(cots)
    step(rows)
    step(by_y)
    step(by_z)
    for c in saved:
        c.wait()


def front(tokens, inverse, documents, small, out_weight, gate, up, down, cot, qkv_weight):
    every = lead_of(AXES) + (16, D)
    kv = lead_of(KV_DIMS) + (TOK, 512)
    ffn = jax.ShapeDtypeStruct(lead_of(FFN_DIMS) + (ROWS, D), BF)
    rows = jax.ShapeDtypeStruct(lead_of(ROW_DIMS) + (TOK, D), BF)
    copies = count_gather(QKV_ORDERS + QKV_ORDERS[:1] + OUT_ORDERS + (ROW_ORDER, ROW_ORDER))
    copies += count_gather(KEY_ORDERS + 3 * FFN_ORDERS)
    return pl.pallas_call(
        front_kernel,
        out_shape=(
            jax.ShapeDtypeStruct((TOK, D), BF),
            jax.ShapeDtypeStruct((16, D), F32),
            jax.ShapeDtypeStruct((TOK, HQ), BF),
            jax.ShapeDtypeStruct((TOK, HQ), F32),
            jax.ShapeDtypeStruct((TOK, 2048), BF),
            jax.ShapeDtypeStruct((KVH, 8, GQ), F32),
            jax.ShapeDtypeStruct((TOK, D), F32),
            jax.ShapeDtypeStruct((TOK, HD), F32),
            jax.ShapeDtypeStruct((TOK, HD), F32),
            jax.ShapeDtypeStruct((1, TOK), jnp.int32),
            jax.ShapeDtypeStruct(kv, BF),
            jax.ShapeDtypeStruct(every, BF),
            jax.ShapeDtypeStruct(every, BF),
            ffn,
            ffn,
            ffn,
            rows,
            rows,
        ),
        in_specs=[VMEM] * 9 + [ANY],
        out_specs=(VMEM,) * 10 + (ANY,) * 8,
        scratch_shapes=[
            pltpu.VMEM(lead_of(AXES) + (16, 128), BF),
            pltpu.VMEM(every, BF),
            pltpu.VMEM(every, BF),
            pltpu.VMEM(kv, BF),
            pltpu.VMEM((16, D), BF),
            pltpu.VMEM((ROWS, D), BF),
            pltpu.VMEM((ROWS, D), BF),
            pltpu.VMEM((ROWS, D), BF),
            pltpu.VMEM((TOK, HQ), F32),
            pltpu.VMEM((TOK, 512), BF),
            pltpu.VMEM((KVH, GQ, HD), BF),
            pltpu.VMEM((KVH, HD, GQ), F32),
            pltpu.VMEM((KVH, 8, GQ), F32),
            pltpu.VMEM((TOK, D), BF),
            pltpu.SemaphoreType.DMA((copies,)),
            pltpu.SemaphoreType.DMA((copies,)),
            pltpu.SemaphoreType.DMA((12,)),
        ],
        compiler_params=pltpu.CompilerParams(
            collective_id=2, has_side_effects=True, vmem_limit_bytes=56 * 2**20
        ),
    )(tokens, inverse, documents, small, out_weight, gate, up, down, cot, qkv_weight)


def grad_all(kv, qs, gs, lse, delta, first, row, blocks, query_grad, kv_grad):
    query_grad[...] = jnp.zeros_like(query_grad)

    def body(b, edge):
        at = (lax.div(b, 2), pl.ds(lax.rem(b, 2) * 2, 2), slice(None), slice(None))
        allowed = allowed_keys(b, first, row) if edge else None
        later = jnp.where(first > b * KEYS, 1e30, 0.0)
        for g in range(KVH):
            keys = key_block_of(kv, b, head(g))
            values = key_block_of(kv, b, head(2 + g))
            raw = mm(keys, qs[g], (1, 1)) * TO_LOG2
            if edge:
                probs = jnp.where(allowed, jnp.exp2(raw - lse[g, 0:1]), 0.0)
            else:
                probs = jnp.exp2(raw - (lse[g, 0:1] + later))
            prob_grad = mm(values, gs[g], (1, 1))
            score_grad = (probs * (prob_grad - delta[g : g + 1])).astype(BF)
            key_term = mm(score_grad, qs[g], (1, 0)) * SCALE
            value_term = mm(probs.astype(BF), gs[g], (1, 0))
            kv_grad[at + (head(g),)] = key_term.astype(BF).reshape(2, 2, TOK, HD)
            kv_grad[at + (head(2 + g),)] = value_term.astype(BF).reshape(2, 2, TOK, HD)
            query_grad[g] += mm(keys.T, score_grad, (1, 0))

    over_key_blocks(blocks, body)


def collect_row(row, offset, width):
    count = row.shape[1]
    f = lax.broadcasted_iota(jnp.int32, (1, count), 1).astype(F32)
    block = jnp.floor((f + 0.5) * (1.0 / width))
    lane = offset + f - block * width
    index = lax.broadcasted_iota(jnp.int32, (128, count), 0).astype(F32)
    spread = jnp.where(index == block, row, 0.0).astype(BF)
    return mm(spread, (index == lane).astype(BF), (1, 1))


def back_kernel(*refs):
    kv, queries, attended, grad_slots, lse, first_ref, cosine, sine = refs[:8]
    tokens, normed_one, gains, middle, middle_grad, gain_two_grad = refs[8:14]
    gate_part, up_part, down_a, down_b, out_part, ffn_rows, w_qkv = refs[14:21]
    layer_out, input_grad, qkv_out, small_out, out_last, gate_last, up_last, down_last = refs[21:29]
    qkv_part = refs[29]
    qs, gs, delta, query_grad, kv_grad, kv_out, qkv_grad, weight, staged = refs[30:39]
    small, ffn_total, out_out, gate_out, up_out, down_out, free, send, recv, local = refs[39:49]
    scratch = list(refs[49:])
    total = input_grad

    def take(n):
        return [scratch.pop(0) for _ in range(n)]

    me = here()
    links = Links(me, send, recv)
    used = [0]

    def slot():
        used[0] += 1
        return local.at[used[0] - 1]

    def fetch(j):
        c = pltpu.make_async_copy(w_qkv.at[pl.ds(512 * j, 512)], weight.at[j % 2], slot())
        c.start()
        return c

    fetched = [fetch(0), fetch(1)]
    greet(me, ("zh", "x", "y", "z", "c"))
    shared = [take(8) for _ in THIRDS]
    outs = [
        scatter_stream(links, slot(), out_part, AXES, tail, order, part, out_out.at[tail], 16, 16)
        for order, tail, part in zip(ALL_ORDERS, THIRDS, shared, strict=True)
    ]
    rows = [
        scatter_stream(
            links, slot(), ffn_rows, ROW_DIMS, (), ("c", "x"), take(4), ffn_total, TOK, 16
        )
    ]
    gates, ups = (
        [
            scatter_stream(
                links, slot(), source, FFN_DIMS, tail, order, take(4), target.at[tail], ROWS, ROWS
            )
            for order, tail in zip(THIRD_ORDERS, THIRDS, strict=True)
        ]
        for source, target in ((gate_part, gate_out), (up_part, up_out))
    )
    downs = [
        scatter_stream(
            links,
            slot(),
            source,
            rest_of(FFN_DIMS, order[0]),
            (),
            order[1:],
            take(2),
            down_out.at[tail],
            ROWS,
            16,
        )
        for source, order, tail in zip((down_a, down_b), FFN_ORDERS, HALVES, strict=True)
    ]
    step(outs)
    step(rows)
    step(downs)
    blocks, row = key_blocks()
    first = jnp.concatenate([first_ref[...]] * GROUP, axis=1)
    spread = slot_matrix(out_last.shape[0])
    for i in range(4):
        part = mm(grad_slots[:, 512 * i : 512 * (i + 1)], spread, (1, 1))
        for j in range(3):
            h = 3 * i + j
            one = part[:, head(j)]
            gs[h // GROUP, (h % GROUP) * TOK : (h % GROUP + 1) * TOK, :] = one.astype(BF)
            both = (one * attended[:, head(h)]).T
            delta[h // GROUP : h // GROUP + 1, head(h % GROUP)] = jnp.sum(
                both, axis=0, keepdims=True
            )
            qs[h // GROUP, (h % GROUP) * TOK : (h % GROUP + 1) * TOK, :] = queries[:, head(h)]

    def clear(b, carry):
        at = (lax.div(b, 2), pl.ds(lax.rem(b, 2) * 2, 2))
        kv_grad[at] = jnp.zeros((2, 2, TOK, 512), BF)
        return carry

    lax.fori_loop(blocks, 8, clear, 0)
    step(outs)
    step(gates)
    cos, sin = cosine[...], sine[...]
    grad_all(kv, qs, gs, lse, delta, first, row, blocks, query_grad, kv_grad)
    keys = []
    for half, order in enumerate(KV_ORDERS):
        tail = (slice(None), slice(256 * half, 256 * (half + 1)))
        keys.append(
            scatter_stream(
                links, None, kv_grad, KV_DIMS, tail, order, take(6), kv_out.at[half], TOK, 64
            )
        )
    step(outs)
    step(keys)
    for g in range(KVH):
        for i in range(GROUP):
            one = query_grad[g, :, head(i)].T * SCALE
            qkv_grad[:, head(GROUP * g + i)] = (one * cos - turned(one) * sin).astype(BF)
    step(ups[1:2])
    stored = []

    def weight_terms(j):
        if j >= 2:
            stored[j - 2].wait()
        part = qkv_grad[:, 512 * j : 512 * (j + 1)]
        lhs = jnp.concatenate(
            [part[:, head(i)].astype(F32).T.astype(BF) for i in range(4)], axis=0
        )
        for i in range(3):
            cols = slice(512 * i, 512 * (i + 1))
            grad = mm(lhs, normed_one[:, cols], (1, 0)).astype(BF)
            staged[j % 2, :, :, :, :, cols] = grad.reshape(4, 4, 2, 16, 512)
        c = pltpu.make_async_copy(staged.at[j % 2], qkv_part.at[j // 2, j % 2], slot())
        c.start()
        stored.append(c)

    def input_terms(j):
        fetched[j].wait()
        part = qkv_grad[:, 512 * j : 512 * (j + 1)]
        for i in range(3):
            cols = slice(512 * i, 512 * (i + 1))
            term = mm(part, weight[j % 2, :, cols], (1, 0))
            if j == 0:
                total[:, cols] = term
            else:
                total[:, cols] += term

    for j in range(3):
        weight_terms(j)
        input_terms(j)
        if j < 2:
            fetched.append(fetch(j + 2))
    step(keys)
    step(outs)
    step(rows)
    step(keys)
    step(gates)
    step(ups[:1])
    step(ups[2:])
    step(outs)
    for axis in ("c", "x", "y", "z"):
        for k in REACH[axis]:
            pl.semaphore_signal(
                free,
                inc=1,
                device_id=device_id(peer(me, axis, k)),
                device_id_type=pl.DeviceIdType.MESH,
            )
    step(keys)
    for g in range(KVH):
        one = kv_out[0, :, head(g)]
        qkv_grad[:, head(H + g)] = (one * cos - turned(one) * sin).astype(BF)
        qkv_grad[:, head(H + 2 + g)] = kv_out[1, :, head(g)].astype(BF)
    weight_terms(3)
    for c in stored[2:]:
        c.wait()
    pl.semaphore_wait(free, 10)
    qkvs = [
        scatter_stream(links, slot(), qkv_part, AXES, tail, order, part, qkv_out.at[tail], 16, 16)
        for order, tail, part in zip(ALL_ORDERS, THIRDS, shared, strict=True)
    ]
    step(qkvs)
    input_terms(3)
    whole = tokens[...].astype(F32)
    factor = lax.rsqrt(jnp.sum(whole * whole, axis=1, keepdims=True) / D + norm_eps)
    grad = total[...]
    gain_one_grad = jnp.sum(grad * whole * factor, axis=0, keepdims=True)
    bias_grad = jnp.sum(qkv_grad[...].astype(F32), axis=0, keepdims=True)
    line = lax.broadcasted_iota(jnp.int32, (128, 16, 128), 1)
    blocks_grad = jnp.zeros((128, 16, 128), F32)
    for i, (one, width) in enumerate(
        ((gain_one_grad, 12), (gain_two_grad[0:1], 12), (bias_grad, 16))
    ):
        blocks_grad = jnp.where(line == i, collect_row(one, 0, width)[:, None, :], blocks_grad)
    small[...] = blocks_grad.astype(BF).reshape(lead_of(AXES) + (16, 128))
    smalls = [
        scatter_stream(links, None, small, AXES, (), ALL_ORDERS[0], take(8), small_out, 16, 16)
    ]
    step(smalls)
    step(ups[1:2])
    step(qkvs)
    step(smalls)
    step(ups[:1])
    step(ups[2:])
    scaled = grad * gains[0:1]
    mean = jnp.sum(scaled * whole, axis=1, keepdims=True) / D
    input_grad[...] = middle_grad[...] + factor * scaled - whole * (factor * factor * factor * mean)
    step(rows)
    layer_out[...] = (middle[...] + ffn_total[...]).astype(BF)
    step(downs)
    step(gates)
    step(qkvs)
    step(smalls)
    step(ups)
    step(qkvs)
    step(smalls)
    out_last[...] = out_out[0 : out_last.shape[0]]
    units = gate_last.shape[0]
    gate_last[...] = gate_out[0:units]
    down_last[...] = down_out[0:units]
    up_last[...] = up_out[0:units]
    step(qkvs)
    step(smalls)


def back(inputs, parts, w_qkv, out_rows, units):
    copies = count_scatter(KV_ORDERS) + 2 * count_scatter(ALL_ORDERS)
    copies += count_scatter(ALL_ORDERS[:1]) + count_scatter([("c", "x")])
    copies += 2 * count_scatter(THIRD_ORDERS) + count_scatter(LAST_STAGE)
    every = lead_of(AXES) + (16, D)
    scratch = []
    for order in ALL_ORDERS:
        scratch += scatter_scratch(AXES, order, 16, 512)
    scratch += scatter_scratch(ROW_DIMS, ("c", "x"), TOK, D)
    for _ in range(2):
        for order in THIRD_ORDERS:
            scratch += scatter_scratch(FFN_DIMS, order, ROWS, 512)
    for order in FFN_ORDERS:
        scratch += scatter_scratch(rest_of(FFN_DIMS, order[0]), order[1:], ROWS, 768)
    for order in KV_ORDERS:
        scratch += scatter_scratch(KV_DIMS, order, TOK, 256)
    scratch += scatter_scratch(AXES, ALL_ORDERS[0], 16, 128)
    ffn = jax.ShapeDtypeStruct((units, D), F32)
    return pl.pallas_call(
        back_kernel,
        out_shape=(
            jax.ShapeDtypeStruct((TOK, D), BF),
            jax.ShapeDtypeStruct((TOK, D), F32),
            jax.ShapeDtypeStruct((16, D), F32),
            jax.ShapeDtypeStruct((16, 128), F32),
            jax.ShapeDtypeStruct((out_rows, D), F32),
            ffn,
            ffn,
            ffn,
            jax.ShapeDtypeStruct(every, BF),
        ),
        in_specs=[VMEM] * 14 + [ANY] * 7,
        out_specs=(VMEM,) * 8 + (ANY,),
        scratch_shapes=[
            pltpu.VMEM((KVH, GQ, HD), BF),
            pltpu.VMEM((KVH, GQ, HD), BF),
            pltpu.VMEM((8, GQ), F32),
            pltpu.VMEM((KVH, HD, GQ), F32),
            pltpu.VMEM(lead_of(KV_DIMS) + (TOK, 512), BF),
            pltpu.VMEM((2, TOK, 256), F32),
            pltpu.VMEM((TOK, 2048), BF),
            pltpu.VMEM((2, 512, D), BF),
            pltpu.VMEM((2, 4, 4, 2, 16, D), BF),
            pltpu.VMEM(lead_of(AXES) + (16, 128), BF),
            pltpu.VMEM((TOK, D), F32),
            pltpu.VMEM((16, D), F32),
            pltpu.VMEM((ROWS, D), F32),
            pltpu.VMEM((ROWS, D), F32),
            pltpu.VMEM((ROWS, D), F32),
            pltpu.SemaphoreType.REGULAR,
            pltpu.SemaphoreType.DMA((copies,)),
            pltpu.SemaphoreType.DMA((copies,)),
            pltpu.SemaphoreType.DMA((38,)),
        ]
        + scratch,
        compiler_params=pltpu.CompilerParams(
            collective_id=5, has_side_effects=True, vmem_limit_bytes=63 * 2**20
        ),
    )(*inputs, *parts, w_qkv)


def results_kernel(*refs):
    small, sources, gain_grads, bias_grad = refs[0], refs[1:8], refs[8], refs[9]
    targets = refs[10:17]
    for src, dst in zip(sources, targets, strict=True):
        dst = dst.at[0] if len(dst.shape) == 3 else dst
        dst[...] = src[...]
    gain_grads[...] = small[0:2, 0 : gain_grads.shape[1]]
    bias_grad[...] = small[2:3, 0 : bias_grad.shape[1]]


def results(small, arrays, gains, features):
    shapes = [(1,) + a.shape if a.shape[0] == TOK else a.shape for a in arrays]
    return pl.pallas_call(
        results_kernel,
        out_shape=(
            jax.ShapeDtypeStruct((2, gains), F32),
            jax.ShapeDtypeStruct((1, features), F32),
            *(jax.ShapeDtypeStruct(n, a.dtype) for n, a in zip(shapes, arrays, strict=True)),
        ),
        in_specs=[VMEM] * 8,
        out_specs=(VMEM,) * 9,
    )(small, *arrays)


def dot(a, b, dims):
    return lax.dot_general(a, b, ((dims[:1], dims[1:]), ((), ())), preferred_element_type=F32)


def local(
    tokens_in,
    qkv_weight,
    qkv_bias,
    out_weight,
    norm_gains,
    gate_weight,
    up_weight,
    down_weight,
    doc_ids,
    cotangent,
):
    cot_low = cotangent[0]

    small = jnp.concatenate([qkv_bias, norm_gains.reshape(-1)])[None]
    small = jnp.pad(small, ((0, 15), (0, 128 - small.shape[1])))
    units, out_rows = gate_weight.shape[0], out_weight.shape[0]
    inverse = rope_base ** (-(jnp.arange(HD // 2, dtype=jnp.float32) * 2.0 / HD))
    inverse = jnp.concatenate([inverse, inverse])[None]
    (
        normed_one,
        gains,
        queries,
        attended,
        slots,
        lse,
        middle,
        cosine,
        sine,
        first,
        kv,
        w_qkv,
        w_out,
        w_gate,
        w_up,
        w_down,
        cot_rows,
        rows_two,
    ) = front(
        tokens_in[0],
        inverse,
        doc_ids,
        small,
        out_weight,
        gate_weight,
        up_weight,
        down_weight,
        cot_low,
        qkv_weight,
    )
    w_qkv = w_qkv.reshape(2048, D)
    w_out = w_out.reshape(2048, D)
    w_gate, w_up, w_down = (w.reshape(-1, D) for w in (w_gate, w_up, w_down))
    cot_rows, rows_two = cot_rows.reshape(-1, D), rows_two.reshape(-1, D)

    gate = dot(w_gate, rows_two, (1, 1)).astype(BF)
    upward = dot(w_up, rows_two, (1, 1)).astype(BF)
    gate, upward = (v.astype(F32) for v in lax.optimization_barrier((gate, upward)))
    hidden_grad = dot(w_down, cot_rows, (1, 1))
    sigma = jax.nn.sigmoid(gate)
    hidden = (gate * sigma * upward).astype(BF)
    gate_grad = (hidden_grad * upward * sigma * (1.0 + gate * (1.0 - sigma))).astype(BF)
    upward_grad = (hidden_grad * gate * sigma).astype(BF)
    ffn_part = dot(hidden, w_down, (0, 0)).astype(BF)
    grad_part = (dot(gate_grad, w_gate, (0, 0)) + dot(upward_grad, w_up, (0, 0))).astype(BF)
    rows_lead = lead_of(ROW_DIMS) + (TOK, D)
    middle_grad, gain_two_grad, grad_slots, down_a, down_b, gate_part, up_part, out_part = scatter_rows(
        (middle, cot_low, gains, slots),
        grad_part.reshape(rows_lead),
        rows_two,
        cot_rows,
        hidden,
        gate_grad,
        upward_grad,
        w_out,
    )
    layer_out, input_grad, qkv_sum, small_sum, out_sum, gate_sum, up_sum, down_sum, _ = back(
        (
            kv,
            queries,
            attended,
            grad_slots,
            lse,
            first,
            cosine,
            sine,
            tokens_in[0],
            normed_one,
            gains,
            middle,
            middle_grad,
            gain_two_grad,
        ),
        (gate_part, up_part, down_a, down_b, out_part, ffn_part.reshape(rows_lead)),
        w_qkv,
        out_rows,
        units,
    )
    gain_grads, bias_grad, *arrays = results(
        small_sum,
        (layer_out, input_grad, qkv_sum, out_sum, gate_sum, up_sum, down_sum),
        norm_gains.shape[1],
        qkv_bias.shape[0],
    )
    return (*arrays[:3], bias_grad[0], arrays[3], gain_grads, *arrays[4:])


def solution(mesh):
    fine = Mesh(mesh.devices.reshape(tuple(SIZE[a] for a in AXES)), AXES)
    dp, ctx = ("zl", "c"), ("y", "x", "zh")
    in_specs = (
        P(dp, ctx, None),
        P(AXES, None),
        P(AXES),
        P(AXES, None),
        P(None, AXES),
        P(AXES, None),
        P(AXES, None),
        P(AXES, None),
        P(dp, None),
        P(dp, ctx, None),
    )
    out_specs = (
        P(dp, ctx, None),
        P(dp, ctx, None),
        P(AXES, None),
        P(AXES),
        P(AXES, None),
        P(None, AXES),
        P(AXES, None),
        P(AXES, None),
        P(AXES, None),
    )
    return jax.shard_map(local, mesh=fine, in_specs=in_specs, out_specs=out_specs, check_vma=False)
```

profile of v0, /device:TPU:0, one launch (start us, length us, event | category | flops | bytes accessed | tf_op | source)
XLA Modules:
  0.0 328.5 jit_solution(64922126326175205)
XLA Ops:
  0.6 0.7 reshape.48
  1.4 0.7 maximum_bitcast_fusion.1
  2.1 0.6 maximum_bitcast_fusion.refs_1_
  2.7 0.6 pad.4.refs_3_
  3.3 121.0 %shard_map.169 = (bf16[128,1536]{1,0:T(8,128)(2,1)}, f32[16,1536]{1,0:T(8,128)}, bf16[128,1536]{1,0:T(8,128)(2,1)}, f32[128,1536]{1,0:T(8,128)}, bf16[128,2048]{...) custom-call(bf16[128,1536]{1,0:T(8,128)(2,1)} %bitcast.37, ...), custom_call_target="tpu_custom_call" | custom-call | tf_op jit(solution)/shard_map/pallas_call | solution.py:704
  124.3 0.0 copy-start.1
  124.3 0.0 copy-start.5
  124.3 7.5 %convolution_convert_fusion.1 = bf16[1280,1024]{1,0:T(8,128)(2,1)S(1)} fusion(bf16[1280,1536]{1,0:T(8,128)(2,1)} %bitcast.43, bf16[1024,1536]{1,0:T(8,128)(2,1)} %bitcast.33), kind=kOutput, calls=%fused_computation.18 | convolution fusion | flops 4027842560 | bytes 9699328 | tf_op jit(solution)/shard_map/dot_general | solution.py:1087
  131.8 0.0 copy-done.1
  131.8 0.0 copy-done.5
  131.8 0.0 copy-start
  131.9 0.0 copy-start.7
  131.9 4.8 %convolution_convert_fusion = bf16[1280,1024]{1,0:T(8,128)(2,1)S(1)} fusion(bf16[1280,1536]{1,0:T(8,128)(2,1)S(1)} %bitcast.41, bf16[1024,1536]{1,0:T(8,128)(2,1)S(1)} %bitcast.35), kind=kOutput, calls=%fused_computation.17 | convolution fusion | flops 4027842560 | bytes 9699328 | tf_op jit(solution)/shard_map/dot_general | solution.py:1087
  136.6 0.0 copy-done
  136.7 0.0 copy-done.7
  136.7 7.1 %fusion.9 = (bf16[1280,1024]{1,0:T(8,128)(2,1)S(1)}, bf16[1280,1024]{1,0:T(8,128)(2,1)S(1)}, bf16[1280,1024]{1,0:T(8,128)(2,1)S(1)}) fusion(bf16[1280,1024]{1,0:T(8,128)(2,1)S(1)} %convolution_convert_fusion.1, bf16[1280,1024]{1,0:T(8,128)(2,1)S(1)} %convolution_convert_fusion, bf16[1280,1536]{1,0:T(8,128)(2,1)S(1)} %bitcast.45, ...), kind=kOutput, calls=%fused_computation.16 | convolution fusion | flops 4050124800 | bytes 20185088 | tf_op jit(solution)/shard_map/dot_general | solution.py:1087
  143.8 0.0 copy-start.4
  143.8 0.0 copy-start.3
  143.8 0.0 copy-start.2
  143.8 0.0 copy-start.6
  143.8 5.9 %convolution_convert_fusion.2 = bf16[1024,1536]{1,0:T(8,128)(2,1)} fusion(bf16[1280,1024]{1,0:T(8,128)(2,1)S(1)} %get-tuple-element.101.refs_7_, bf16[1280,1536]{1,0:T(8,128)(2,1)S(1)} %bitcast.46), kind=kOutput, calls=%fused_computation.19 | convolution fusion | flops 4028104704 | bytes 9699328 | tf_op jit(solution)/shard_map/dot_general | solution.py:1087
  149.8 0.0 copy-done.4
  149.8 0.0 copy-done.3
  149.8 0.0 copy-done.6
  149.8 4.4 %fusion.10 = f32[1024,1536]{1,0:T(8,128)S(1)} fusion(bf16[1280,1024]{1,0:T(8,128)(2,1)S(1)} %get-tuple-element.100.refs_8_, bf16[1280,1536]{1,0:T(8,128)(2,1)S(1)} %bitcast.44), kind=kOutput, calls=%fused_computation.23 | convolution fusion | flops 4026531840 | bytes 12845056 | tf_op jit(solution)/shard_map/dot_general | solution.py:1087
  154.2 0.0 copy-done.2
  154.2 6.3 %add_convert_fusion = bf16[1024,1536]{1,0:T(8,128)(2,1)} fusion(f32[1024,1536]{1,0:T(8,128)S(1)} %fusion.10, bf16[1280,1024]{1,0:T(8,128)(2,1)S(1)} %get-tuple-element.99.refs_9_, bf16[1280,1536]{1,0:T(8,128)(2,1)S(1)} %bitcast.42), kind=kOutput, calls=%fused_computation.6 | convolution fusion | flops 4029677568 | bytes 15990784 | tf_op jit(solution)/shard_map/dot_general | solution.py:1087
  160.6 36.6 %shard_map.170 = (f32[128,1536]{1,0:T(8,128)}, f32[1,1536]{1,0:T(1,128)}, bf16[128,2048]{1,0:T(8,128)(2,1)}, bf16[2,2,80,768]{3,2,1,0:T(8,128)(2,1)}, bf16[4,80,...) custom-call(f32[128,1536]{1,0:T(8,128)} %get-tuple-element.57.refs_0, ...), custom_call_target="tpu_custom_call" | custom-call | tf_op jit(solution)/shard_map/pallas_call | solution.py:396
  197.2 127.5 %shard_map.171 = (bf16[128,1536]{1,0:T(8,128)(2,1)}, f32[128,1536]{1,0:T(8,128)}, f32[16,1536]{1,0:T(8,128)}, f32[16,128]{1,0:T(8,128)}, f32[12,1536]{1,0:T(8,12...) custom-call(bf16[4,4,2,128,512]{4,3,2,1,0:T(8,128)(2,1)} %get-tuple-, ...), custom_call_target="tpu_custom_call" | custom-call | tf_op jit(solution)/shard_map/pallas_call | solution.py:1019
  324.7 3.3 %shard_map.172 = (f32[2,12]{1,0:T(2,128)}, f32[1,16]{1,0:T(1,128)}, bf16[1,128,1536]{2,1,0:T(8,128)(2,1)}, f32[1,128,1536]{2,1,0:T(8,128)}, f32[16,1536]{1,0:T(8...) custom-call(f32[16,128]{1,0:T(8,128)} %get-tuple-element.82.refs_0_, ...), custom_call_target="tpu_custom_call" | custom-call | tf_op jit(solution)/shard_map/pallas_call | solution.py:1074
  (1 shorter events, 0.0 us)
Async XLA Ops:
  124.3 7.5 %copy-start.1 = (bf16[4,2,128,1536]{3,2,1,0:T(8,128)(2,1)S(1)}, bf16[4,2,128,1536]{3,2,1,0:T(8,128)(2,1)}, u32[]{:S(2)}) copy-start(bf16[4,2,128,1536]{3,2,1,0:T(8,128)(2,1)} %get-tuple-element.63) | copy-start | bytes 9437188
  124.3 7.5 %copy-start.5 = (bf16[2,4,2,80,1536]{4,3,2,1,0:T(8,128)(2,1)S(1)}, bf16[2,4,2,80,1536]{4,3,2,1,0:T(8,128)(2,1)}, u32[]{:S(2)}) copy-start(bf16[2,4,2,80,1536]{4,3,2,1,0:T(8,128)(2,1)} %get-tuple-element.64) | copy-start | bytes 11796484
  131.8 4.8 %copy-start = (bf16[4,2,128,1536]{3,2,1,0:T(8,128)(2,1)S(1)}, bf16[4,2,128,1536]{3,2,1,0:T(8,128)(2,1)}, u32[]{:S(2)}) copy-start(bf16[4,2,128,1536]{3,2,1,0:T(8,128)(2,1)} %get-tuple-element.61) | copy-start | bytes 9437188
  131.9 4.8 %copy-start.7 = (bf16[2,4,2,80,1536]{4,3,2,1,0:T(8,128)(2,1)S(1)}, bf16[2,4,2,80,1536]{4,3,2,1,0:T(8,128)(2,1)}, u32[]{:S(2)}) copy-start(bf16[2,4,2,80,1536]{4,3,2,1,0:T(8,128)(2,1)} %get-tuple-element.60) | copy-start | bytes 11796484
  143.8 6.0 %copy-start.4 = (bf16[1280,1024]{1,0:T(8,128)(2,1)}, bf16[1280,1024]{1,0:T(8,128)(2,1)S(1)}, u32[]{:S(2)}) copy-start(bf16[1280,1024]{1,0:T(8,128)(2,1)S(1)} %get-tuple-element.101.refs_7_) | copy-start | bytes 7864324
  143.8 6.0 %copy-start.3 = (bf16[1280,1024]{1,0:T(8,128)(2,1)}, bf16[1280,1024]{1,0:T(8,128)(2,1)S(1)}, u32[]{:S(2)}) copy-start(bf16[1280,1024]{1,0:T(8,128)(2,1)S(1)} %get-tuple-element.100.refs_8_) | copy-start | bytes 7864324
  143.8 10.4 %copy-start.2 = (bf16[1280,1024]{1,0:T(8,128)(2,1)}, bf16[1280,1024]{1,0:T(8,128)(2,1)S(1)}, u32[]{:S(2)}) copy-start(bf16[1280,1024]{1,0:T(8,128)(2,1)S(1)} %get-tuple-element.99.refs_9_) | copy-start | bytes 7864324
  143.8 6.0 %copy-start.6 = (bf16[2,4,2,80,1536]{4,3,2,1,0:T(8,128)(2,1)S(1)}, bf16[2,4,2,80,1536]{4,3,2,1,0:T(8,128)(2,1)}, u32[]{:S(2)}) copy-start(bf16[2,4,2,80,1536]{4,3,2,1,0:T(8,128)(2,1)} %get-tuple-element.62) | copy-start | bytes 11796484
where the time goes:
time: 334 us; the launch traced here: 328 us
  Pallas kernels  288 us (86%)
  matrix products  36.1 us (11%)
    pallas_call x1, Pallas kernels, back(): pl.pallas_call(back_kernel, out_shape=(jax.ShapeDtypeStruct((TOK, D), BF)...  128 us
    pallas_call x1, Pallas kernels, front(): pl.pallas_call(front_kernel, out_shape=(jax.ShapeDtypeStruct((TOK, D), BF...  121 us
    pallas_call x1, Pallas kernels, scatter_rows(): pl.pallas_call(rows_scatter_kernel, out_shape=(jax.ShapeDtypeStruct((TOK,...  36.6 us
    dot_general x6, matrix products, dot(): lax.dot_general(a, b, ((dims[:1], dims[1:]), ((), ())), preferred_element...  36.1 us

commit v1 on v0

--- a/solution.py
+++ b/solution.py
@@ -544,7 +544,7 @@
     cosine, sine, first_ref = refs[17:20]
     kv_hbm, qkv_hbm, out_hbm, gate_all, up_all, down_all, cot_all, rows_all = refs[20:28]
     small_all, w_qkv, w_out, kv, out_block, gate, up, down = refs[28:36]
-    qkv, block, qs, acc, stats, normed, send, recv, local = refs[36:]
+    padded, qkv, block, qs, acc, stats, normed, send, recv, local = refs[36:]
     me = here()
     links = Links(me, send, recv)
     own = []
@@ -559,16 +559,14 @@
         keep(small, small_all.at[place(AXES, me, ())]),
         keep(cot, cot_all.at[place(ROW_DIMS, me, ())]),
     ]
+    ffn = ((gate_in, gate, gate_all), (up_in, up, up_all), (down_in, down, down_all))
     out_rows = out_in.shape[0]
-    out_block[0:out_rows] = out_in[...]
-    out_block[out_rows:16] = jnp.zeros((16 - out_rows, D), BF)
-    first_copies.append(keep(out_block, w_out.at[place(AXES, me, ())]))
-    units = gate_in.shape[0]
-    ffn = ((gate_in, gate, gate_all), (up_in, up, up_all), (down_in, down, down_all))
-    for a, b, c in ffn:
-        b[0:units] = a[...]
-        b[units:ROWS] = jnp.zeros((ROWS - units, D), BF)
-        first_copies.append(keep(b, c.at[place(FFN_DIMS, me, ())]))
+
+    def pad_rows(source, target):
+        padded[...] = jnp.zeros_like(padded)
+        padded[0 : source.shape[0]] = source[...].astype(F32)
+        target[...] = padded[0 : target.shape[0]].astype(BF)
+
     greet(me, ("x", "y", "z", "c", "zh"))
     qkvs = [
         gather_stream(links, qkv_block.at[tail], w_qkv, AXES, tail, order)
@@ -588,7 +586,12 @@
     )
     cots = [gather_stream(links, cot, cot_all, ROW_DIMS, (), ROW_ORDER)]
     step(qkvs)
+    pad_rows(out_in, out_block)
+    first_copies.append(keep(out_block, w_out.at[place(AXES, me, ())]))
     step(outs)
+    for a, b, c in ffn:
+        pad_rows(a, b)
+        first_copies.append(keep(b, c.at[place(FFN_DIMS, me, ())]))
     whole = tokens[...].astype(F32)
     factor = lax.rsqrt(jnp.sum(whole * whole, axis=1, keepdims=True) / D + norm_eps)
     first_copies[0].wait()
@@ -734,6 +737,7 @@
             pltpu.VMEM((ROWS, D), BF),
             pltpu.VMEM((ROWS, D), BF),
             pltpu.VMEM((ROWS, D), BF),
+            pltpu.VMEM((ROWS, D), F32),
             pltpu.VMEM((TOK, HQ), F32),
             pltpu.VMEM((TOK, 512), BF),
             pltpu.VMEM((KVH, GQ, HD), BF),

time: 334 us -> 334 us (level)
  no operation moved by 1% of the time
where the time goes in v1:
time: 334 us; the launch traced here: 328 us
  Pallas kernels  288 us (86%)
  matrix products  36.1 us (11%)
    pallas_call x1, Pallas kernels, back(): pl.pallas_call(back_kernel, out_shape=(jax.ShapeDtypeStruct((TOK, D), BF)...  128 us
    pallas_call x1, Pallas kernels, front(): pl.pallas_call(front_kernel, out_shape=(jax.ShapeDtypeStruct((TOK, D), BF...  121 us
    pallas_call x1, Pallas kernels, scatter_rows(): pl.pallas_call(rows_scatter_kernel, out_shape=(jax.ShapeDtypeStruct((TOK,...  36.5 us
    dot_general x6, matrix products, dot(): lax.dot_general(a, b, ((dims[:1], dims[1:]), ((), ())), preferred_element...  36.1 us

profile of v1, /device:TPU:0, one launch (start us, length us, event | category | flops | bytes accessed | tf_op | source)
XLA Modules:
  0.0 328.3 jit_solution(11475169674048145656)
XLA Ops:
  0.6 0.7 reshape.48
  1.4 0.7 maximum_bitcast_fusion.1
  2.1 0.6 maximum_bitcast_fusion.refs_1_
  2.7 0.6 pad.4.refs_3_
  3.3 120.9 %shard_map.169 = (bf16[128,1536]{1,0:T(8,128)(2,1)}, f32[16,1536]{1,0:T(8,128)}, bf16[128,1536]{1,0:T(8,128)(2,1)}, f32[128,1536]{1,0:T(8,128)}, bf16[128,2048]{...) custom-call(bf16[128,1536]{1,0:T(8,128)(2,1)} %bitcast.37, ...), custom_call_target="tpu_custom_call" | custom-call | tf_op jit(solution)/shard_map/pallas_call | solution.py:707
  124.2 0.0 copy-start.1
  124.2 0.0 copy-start.5
  124.2 7.5 %convolution_convert_fusion.1 = bf16[1280,1024]{1,0:T(8,128)(2,1)S(1)} fusion(bf16[1280,1536]{1,0:T(8,128)(2,1)} %bitcast.43, bf16[1024,1536]{1,0:T(8,128)(2,1)} %bitcast.33), kind=kOutput, calls=%fused_computation.18 | convolution fusion | flops 4027842560 | bytes 9699328 | tf_op jit(solution)/shard_map/dot_general | solution.py:1091
  131.7 0.0 copy-done.1
  131.7 0.0 copy-done.5
  131.7 0.0 copy-start
  131.7 0.0 copy-start.7
  131.8 4.8 %convolution_convert_fusion = bf16[1280,1024]{1,0:T(8,128)(2,1)S(1)} fusion(bf16[1280,1536]{1,0:T(8,128)(2,1)S(1)} %bitcast.41, bf16[1024,1536]{1,0:T(8,128)(2,1)S(1)} %bitcast.35), kind=kOutput, calls=%fused_computation.17 | convolution fusion | flops 4027842560 | bytes 9699328 | tf_op jit(solution)/shard_map/dot_general | solution.py:1091
  136.5 0.0 copy-done
  136.5 0.0 copy-done.7
  136.6 7.1 %fusion.9 = (bf16[1280,1024]{1,0:T(8,128)(2,1)S(1)}, bf16[1280,1024]{1,0:T(8,128)(2,1)S(1)}, bf16[1280,1024]{1,0:T(8,128)(2,1)S(1)}) fusion(bf16[1280,1024]{1,0:T(8,128)(2,1)S(1)} %convolution_convert_fusion.1, bf16[1280,1024]{1,0:T(8,128)(2,1)S(1)} %convolution_convert_fusion, bf16[1280,1536]{1,0:T(8,128)(2,1)S(1)} %bitcast.45, ...), kind=kOutput, calls=%fused_computation.16 | convolution fusion | flops 4050124800 | bytes 20185088 | tf_op jit(solution)/shard_map/dot_general | solution.py:1091
  143.7 0.0 copy-start.4
  143.7 0.0 copy-start.3
  143.7 0.0 copy-start.2
  143.7 0.0 copy-start.6
  143.7 5.9 %convolution_convert_fusion.2 = bf16[1024,1536]{1,0:T(8,128)(2,1)} fusion(bf16[1280,1024]{1,0:T(8,128)(2,1)S(1)} %get-tuple-element.101.refs_7_, bf16[1280,1536]{1,0:T(8,128)(2,1)S(1)} %bitcast.46), kind=kOutput, calls=%fused_computation.19 | convolution fusion | flops 4028104704 | bytes 9699328 | tf_op jit(solution)/shard_map/dot_general | solution.py:1091
  149.7 0.0 copy-done.4
  149.7 0.0 copy-done.3
  149.7 0.0 copy-done.6
  149.7 4.4 %fusion.10 = f32[1024,1536]{1,0:T(8,128)S(1)} fusion(bf16[1280,1024]{1,0:T(8,128)(2,1)S(1)} %get-tuple-element.100.refs_8_, bf16[1280,1536]{1,0:T(8,128)(2,1)S(1)} %bitcast.44), kind=kOutput, calls=%fused_computation.23 | convolution fusion | flops 4026531840 | bytes 12845056 | tf_op jit(solution)/shard_map/dot_general | solution.py:1091
  154.1 0.0 copy-done.2
  154.1 6.3 %add_convert_fusion = bf16[1024,1536]{1,0:T(8,128)(2,1)} fusion(f32[1024,1536]{1,0:T(8,128)S(1)} %fusion.10, bf16[1280,1024]{1,0:T(8,128)(2,1)S(1)} %get-tuple-element.99.refs_9_, bf16[1280,1536]{1,0:T(8,128)(2,1)S(1)} %bitcast.42), kind=kOutput, calls=%fused_computation.6 | convolution fusion | flops 4029677568 | bytes 15990784 | tf_op jit(solution)/shard_map/dot_general | solution.py:1091
  160.4 36.5 %shard_map.170 = (f32[128,1536]{1,0:T(8,128)}, f32[1,1536]{1,0:T(1,128)}, bf16[128,2048]{1,0:T(8,128)(2,1)}, bf16[2,2,80,768]{3,2,1,0:T(8,128)(2,1)}, bf16[4,80,...) custom-call(f32[128,1536]{1,0:T(8,128)} %get-tuple-element.57.refs_0, ...), custom_call_target="tpu_custom_call" | custom-call | tf_op jit(solution)/shard_map/pallas_call | solution.py:396
  197.0 127.5 %shard_map.171 = (bf16[128,1536]{1,0:T(8,128)(2,1)}, f32[128,1536]{1,0:T(8,128)}, f32[16,1536]{1,0:T(8,128)}, f32[16,128]{1,0:T(8,128)}, f32[12,1536]{1,0:T(8,12...) custom-call(bf16[4,4,2,128,512]{4,3,2,1,0:T(8,128)(2,1)} %get-tuple-, ...), custom_call_target="tpu_custom_call" | custom-call | tf_op jit(solution)/shard_map/pallas_call | solution.py:1023
  324.5 3.3 %shard_map.172 = (f32[2,12]{1,0:T(2,128)}, f32[1,16]{1,0:T(1,128)}, bf16[1,128,1536]{2,1,0:T(8,128)(2,1)}, f32[1,128,1536]{2,1,0:T(8,128)}, f32[16,1536]{1,0:T(8...) custom-call(f32[16,128]{1,0:T(8,128)} %get-tuple-element.82.refs_0_, ...), custom_call_target="tpu_custom_call" | custom-call | tf_op jit(solution)/shard_map/pallas_call | solution.py:1078
  (1 shorter events, 0.0 us)
Async XLA Ops:
  124.2 7.5 %copy-start.1 = (bf16[4,2,128,1536]{3,2,1,0:T(8,128)(2,1)S(1)}, bf16[4,2,128,1536]{3,2,1,0:T(8,128)(2,1)}, u32[]{:S(2)}) copy-start(bf16[4,2,128,1536]{3,2,1,0:T(8,128)(2,1)} %get-tuple-element.63) | copy-start | bytes 9437188
  124.2 7.5 %copy-start.5 = (bf16[2,4,2,80,1536]{4,3,2,1,0:T(8,128)(2,1)S(1)}, bf16[2,4,2,80,1536]{4,3,2,1,0:T(8,128)(2,1)}, u32[]{:S(2)}) copy-start(bf16[2,4,2,80,1536]{4,3,2,1,0:T(8,128)(2,1)} %get-tuple-element.64) | copy-start | bytes 11796484
  131.7 4.8 %copy-start = (bf16[4,2,128,1536]{3,2,1,0:T(8,128)(2,1)S(1)}, bf16[4,2,128,1536]{3,2,1,0:T(8,128)(2,1)}, u32[]{:S(2)}) copy-start(bf16[4,2,128,1536]{3,2,1,0:T(8,128)(2,1)} %get-tuple-element.61) | copy-start | bytes 9437188
  131.7 4.8 %copy-start.7 = (bf16[2,4,2,80,1536]{4,3,2,1,0:T(8,128)(2,1)S(1)}, bf16[2,4,2,80,1536]{4,3,2,1,0:T(8,128)(2,1)}, u32[]{:S(2)}) copy-start(bf16[2,4,2,80,1536]{4,3,2,1,0:T(8,128)(2,1)} %get-tuple-element.60) | copy-start | bytes 11796484
  143.7 6.0 %copy-start.4 = (bf16[1280,1024]{1,0:T(8,128)(2,1)}, bf16[1280,1024]{1,0:T(8,128)(2,1)S(1)}, u32[]{:S(2)}) copy-start(bf16[1280,1024]{1,0:T(8,128)(2,1)S(1)} %get-tuple-element.101.refs_7_) | copy-start | bytes 7864324
  143.7 6.0 %copy-start.3 = (bf16[1280,1024]{1,0:T(8,128)(2,1)}, bf16[1280,1024]{1,0:T(8,128)(2,1)S(1)}, u32[]{:S(2)}) copy-start(bf16[1280,1024]{1,0:T(8,128)(2,1)S(1)} %get-tuple-element.100.refs_8_) | copy-start | bytes 7864324
  143.7 10.4 %copy-start.2 = (bf16[1280,1024]{1,0:T(8,128)(2,1)}, bf16[1280,1024]{1,0:T(8,128)(2,1)S(1)}, u32[]{:S(2)}) copy-start(bf16[1280,1024]{1,0:T(8,128)(2,1)S(1)} %get-tuple-element.99.refs_9_) | copy-start | bytes 7864324
  143.7 6.0 %copy-start.6 = (bf16[2,4,2,80,1536]{4,3,2,1,0:T(8,128)(2,1)S(1)}, bf16[2,4,2,80,1536]{4,3,2,1,0:T(8,128)(2,1)}, u32[]{:S(2)}) copy-start(bf16[2,4,2,80,1536]{4,3,2,1,0:T(8,128)(2,1)} %get-tuple-element.62) | copy-start | bytes 11796484
